TPU v7x, 256 devices: a whole 4x4x8 slice. The times are simulated.
256 devices in a mesh: col: 8 (over z_hi, x), row: 32 (over z_lo, y, core).
Axes of the slice: x: 4, y: 4, z: 8 (z_hi: 2, z_lo: 4; z = z_hi * 4 + z_lo), core: 2. Of those that a mesh axis runs over, the one named last changes fastest.
Arguments:
- trial_states: float32 [16, 2, 131072], P('col', None, 'row'), may hold values from -6 to 6
- resident: bfloat16 [128, 2, 131072], P('col', None, 'row'), may hold values from -6 to 6
- potential: float32 [128, 128, 128], P('row'), may hold values from -1 to 2
- stick_columns: int32 [4096], P('row'), may hold values from 0 to 16383, as said below
- gvector_cells: int32 [131072], P('row'), may hold values from 0 to 16383, as said below
- slab_owner: int32 [32], replicated, may hold values from 0 to 31, each once
- panel_owner: int32 [8], replicated, may hold values from 0 to 7, as said below
- rotation: bfloat16 [128, 128], P(None, 'col'), may hold values from -0.5 to 0.5
Outputs:
- applied: float32 [16, 2, 131072], P('col', None, 'row')
- rotated: bfloat16 [128, 2, 131072], P('col', None, 'row')
Inputs may be any that keep to these rules, and one draw needn't show every extreme that they name: `stick_columns`: the 4096 entries are distinct grid columns. `gvector_cells`: within each row's block of 4096 entries the cells are distinct. `panel_owner`: every column group owns at least one panel.
All inputs are finite; a program needn't handle non-finite values.
Results may differ from a plain program's by a relative error of at most 0.0034.
Values may be sent and summed in bfloat16 or wider, within the bound.
A program may use at most 128 MiB of HBM per device.

v0:
```python
import jax
import jax.numpy as jnp
import numpy as np
from jax import lax
from jax.experimental import pallas as pl
from jax.experimental.pallas import tpu as pltpu
from jax.sharding import PartitionSpec as P

NG = 128
ROWS = 32
XS = 4
CH = 4
GR = 4
MESH = pl.DeviceIdType.MESH
F32 = jnp.float32
BF = jnp.bfloat16
NT = (((1,), (1,)), ((), ()))


def dot(a, b):
    return jnp.dot(a, b, preferred_element_type=F32)


def dot_nt(a, b):
    return lax.dot_general(a, b, NT, preferred_element_type=F32)


def onehot(key, size):
    rows = lax.broadcasted_iota(jnp.int32, (size, key.shape[-1]), 0)
    return jnp.where(rows == key, 1.0, 0.0).astype(BF)


def frequency(j):
    return jnp.where(j < NG // 2, j, j - NG).astype(F32)


def tables():
    phase = 2.0 * np.pi / NG * (np.outer(np.arange(NG), np.arange(NG)) % NG)
    c, s = np.cos(phase), np.sin(phase)
    base = np.block([[c, -s], [s, c]])
    return jnp.asarray(np.stack([base, base.T]), BF)


def kernel(
    trial, resident, potential, columns, cells, slab, owner, rotation, table,
    applied, rotated,
    all_columns, stick_hot, plane_hot, kinetic, sent1, got1, sent2, got2,
    grid, picked, panels, own_part, part_out, part_in, weight_out, weight_in,
    col_send, col_recv, s1, r1, s2, r2, xs, xr, zs, zr, ws, wr,
):
    col = lax.axis_index("col")
    row = lax.axis_index("row")
    half = col // XS
    x = lax.rem(col, XS)
    mate = lax.rem(col + XS, 2 * XS)
    npw = cells.shape[-1]
    width = npw // CH

    def x_peer(d):
        return half * XS + lax.rem(x + d, XS)

    barrier = pltpu.get_barrier_semaphore()

    def greet(d, carry):
        pl.semaphore_signal(
            barrier, inc=1, device_id=(col, lax.rem(row + d, ROWS)), device_id_type=MESH
        )
        return carry

    lax.fori_loop(1, ROWS, greet, 0)
    for d in range(1, XS):
        pl.semaphore_signal(barrier, inc=1, device_id=(x_peer(d), row), device_id_type=MESH)
    pl.semaphore_signal(barrier, inc=1, device_id=(mate, row), device_id_type=MESH)

    for c in range(CH):
        block = resident[:, :, c * width:(c + 1) * width].reshape(32, width)
        panels[c, pl.ds(x, 1)] = block[None]

    lane = lax.broadcasted_iota(jnp.int32, (16, NG), 1)
    sub = lax.broadcasted_iota(jnp.int32, (16, NG), 0)
    perm = jnp.concatenate(
        [jnp.where(lane == owner[p] * 16 + sub, 1.0, 0.0) for p in range(8)], axis=0
    ).astype(BF)
    by_group = dot(rotation[...], perm).astype(BF)
    up = jnp.where(
        lax.broadcasted_iota(jnp.int32, (32, 16), 0) // 2
        == lax.broadcasted_iota(jnp.int32, (32, 16), 1), 1.0, 0.0).astype(BF)
    out = jnp.where(
        lax.broadcasted_iota(jnp.int32, (NG, 256), 1) // 2
        == lax.broadcasted_iota(jnp.int32, (NG, 256), 0), 1.0, 0.0).astype(BF)
    spread = dot(dot(up, by_group).astype(BF), out)
    same = (
        lax.broadcasted_iota(jnp.int32, (32, 256), 0) % 2
        == lax.broadcasted_iota(jnp.int32, (32, 256), 1) % 2
    )
    spread = jnp.where(same, spread, 0.0)
    weight_own = jnp.where(half == 0, spread[:, :NG], spread[:, NG:]).astype(BF)
    weight_out[...] = jnp.where(half == 0, spread[:, NG:], spread[:, :NG]).astype(BF)
    all_columns[pl.ds(row, 1)] = columns[...].reshape(1, 1, NG)

    for c in range(8):
        cell = cells[:, c * 512:(c + 1) * 512]
        z = cell // NG
        stick_hot[:, c * 512:(c + 1) * 512] = onehot((z // 64) * NG + cell % NG, 256)

    pl.semaphore_wait(barrier, ROWS - 1 + XS - 1 + 1)

    def send_columns(d, carry):
        pltpu.make_async_remote_copy(
            columns, all_columns.at[row], col_send, col_recv,
            device_id=(col, lax.rem(row + d, ROWS)), device_id_type=MESH,
        ).start()
        return carry

    lax.fori_loop(1, ROWS, send_columns, 0)
    w_copy = pltpu.make_async_remote_copy(
        weight_out, weight_in, ws, wr, device_id=(mate, row), device_id_type=MESH
    )
    w_copy.start()

    def x_copy(c, d):
        return pltpu.make_async_remote_copy(
            panels.at[c, x], panels.at[c, x], xs.at[c, d - 1], xr.at[c, d - 1],
            device_id=(x_peer(d), row), device_id_type=MESH,
        )

    def x_arrival(c, d):
        return pltpu.make_async_remote_copy(
            panels.at[c, x], panels.at[c, lax.rem(x + XS - d, XS)], xs.at[c, d - 1], xr.at[c, d - 1],
            device_id=(x_peer(d), row), device_id_type=MESH,
        )

    for c in range(CH):
        for d in (2, 1, 3):
            x_copy(c, d).start()

    def stick_part(c, acc):
        at = pl.ds(pl.multiple_of(c * 512, 512), 512)
        zh = cells[:, at] // NG % 64
        hit = lax.broadcasted_iota(jnp.int32, (64, 512), 0) == zh
        left = jnp.concatenate(
            [jnp.where(hit, trial[s, p:p + 1, at], 0.0) for s in range(2) for p in range(2)],
            axis=0,
        ).astype(BF)
        return acc + dot_nt(left, stick_hot[:, at])

    filled = lax.fori_loop(0, 8, stick_part, jnp.zeros((256, 256), F32))
    filled = jnp.concatenate(
        [
            jnp.concatenate(
                [filled[(2 * s + p) * 64:(2 * s + p + 1) * 64, u * NG:(u + 1) * NG]
                 for p in range(2) for u in range(2)], axis=0)
            for s in range(2)
        ], axis=1).astype(BF)

    j = lax.broadcasted_iota(jnp.int32, (8, 256), 0)
    k = lax.broadcasted_iota(jnp.int32, (8, 256), 1)
    want = j // 4 * NG + j % 4
    order = jnp.concatenate(
        [jnp.where(k == want + slab[r] * 4, 1.0, 0.0) for r in range(ROWS)], axis=0
    ).astype(BF)
    depth_inverse = dot(order, table[0]).astype(BF)
    depth_forward = dot_nt(table[1], order).astype(BF)
    spread_z = dot(depth_inverse, filled)
    for r in range(ROWS):
        rows = slice(8 * r, 8 * r + 8)
        sent1[r] = jnp.concatenate([spread_z[rows, :NG], spread_z[rows, NG:]], axis=0).astype(BF)

    def exchange(source, target, send_sem, recv_sem):
        def go(d, carry):
            to = lax.rem(row + d, ROWS)
            pltpu.make_async_remote_copy(
                source.at[to], target.at[row], send_sem, recv_sem,
                device_id=(col, to), device_id_type=MESH,
            ).start()
            return carry

        lax.fori_loop(1, ROWS, go, 0)
        pltpu.make_async_copy(source.at[row], target.at[row], recv_sem).start()

    exchange(sent1, got1, s1, r1.at[row // (ROWS // GR)])

    own_col = columns[...]
    fx, fy = frequency(own_col // NG), frequency(own_col % NG)
    rows16 = lax.broadcasted_iota(jnp.int32, (16, NG), 0)
    fxy = jnp.where(rows16 == 0, fx, jnp.where(rows16 == 1, fy, 0.0))
    fxy = jnp.concatenate([fxy, fxy], axis=1).astype(BF)
    for c in range(8):
        at = slice(c * 512, (c + 1) * 512)
        f = dot(fxy, stick_hot[:, at])
        fz = frequency(cells[:, at] // NG)
        kinetic[:, at] = 2.0 * (f[0:1] * f[0:1] + f[1:2] * f[1:2] + fz * fz) / (NG * NG)

    pltpu.make_async_copy(all_columns.at[pl.ds(0, ROWS - 1)], all_columns.at[pl.ds(0, ROWS - 1)], col_recv).wait()
    for c in range(8):
        key = jnp.concatenate([all_columns[4 * c + i] for i in range(4)], axis=1)
        plane_hot[:, c * 512:(c + 1) * 512] = onehot(key // (64 * NG) * NG + key % NG, 256)

    def rotate(c):
        if c == 0:
            w_copy.wait()
        for d in range(1, XS):
            x_arrival(c, d).wait_recv()
        both = jnp.concatenate([weight_own, weight_in[...]], axis=0)
        r = dot(both, panels[c].reshape(4 * 32, width))
        own_part[c] = r[:32]
        part_out[c] = r[32:].astype(BF)
        z_copy(c).start()

    def z_copy(c):
        return pltpu.make_async_remote_copy(
            part_out.at[c], part_in.at[c], zs.at[c], zr.at[c],
            device_id=(mate, row), device_id_type=MESH,
        )

    per = ROWS // GR
    for g in range(GR):
        pltpu.make_async_copy(got1.at[pl.ds(g * per, per)], got1.at[pl.ds(g * per, per)], r1.at[g]).wait()
        key = jnp.concatenate([all_columns[per * g + i] for i in range(per)], axis=1)
        hit = lax.broadcasted_iota(jnp.int32, (64, per * NG), 0) == key // NG % 64
        values = jnp.concatenate([got1[per * g + i] for i in range(per)], axis=1).astype(F32)
        right = plane_hot[:, g * per * NG:(g + 1) * per * NG]
        for m in range(4):
            left = jnp.concatenate(
                [jnp.where(hit, values[4 * m + i:4 * m + i + 1], 0.0) for i in range(4)], axis=0
            ).astype(BF)
            part = dot_nt(left, right)
            if g == 0:
                grid[256 * m:256 * m + 256] = part
            else:
                grid[256 * m:256 * m + 256] += part

    rotate(0)
    forward_x, forward_y = table[0], table[1]
    for s in range(2):
        for q in range(4):
            cp = [(s * 2 + p) * 4 + q for p in range(2)]
            block = jnp.concatenate(
                [grid[i * 64:(i + 1) * 64, u * NG:(u + 1) * NG] for i in cp for u in range(2)],
                axis=0).astype(BF)
            t = dot(table[0], block)
            t = jnp.concatenate([t[:NG], t[NG:]], axis=1).astype(BF)
            t = dot(t, table[1])
            v = potential[q] * (2.0 ** -21)
            t = (t * jnp.concatenate([v, v], axis=1)).astype(BF)
            t = dot(t, table[0])
            t = jnp.concatenate([t[:, :NG], t[:, NG:]], axis=0).astype(BF)
            t = dot(table[1], t).astype(BF)
            for p in range(2):
                picked[cp[p] * 64:(cp[p] + 1) * 64] = jnp.concatenate(
                    [t[p * NG:p * NG + 64], t[p * NG + 64:p * NG + NG]], axis=1)

    rotate(1)

    def pick(n, carry):
        pair = lax.rem(row // 2 + n, ROWS // 2)
        at = pl.ds(pl.multiple_of(pair * 256, 256), 256)
        u = dot(picked[...], plane_hot[:, at])
        key = jnp.concatenate([all_columns[2 * pair], all_columns[2 * pair + 1]], axis=1)
        hit = lax.broadcasted_iota(jnp.int32, (64, 256), 0) == key // NG % 64
        got = jnp.concatenate(
            [jnp.sum(jnp.where(hit, u[i * 64:(i + 1) * 64], 0.0), axis=0, keepdims=True)
             for i in range(16)], axis=0).astype(BF)
        for i in range(2):
            to = 2 * pair + i
            sent2[to] = got[:, i * NG:(i + 1) * NG]

            @pl.when(to != row)
            def _():
                pltpu.make_async_remote_copy(
                    sent2.at[to], got2.at[row], s2, r2,
                    device_id=(col, to), device_id_type=MESH,
                ).start()

        return carry

    lax.fori_loop(0, ROWS // 2, pick, 0)
    pltpu.make_async_copy(sent2.at[row], got2.at[row], r2).start()
    rotate(2)
    rotate(3)

    pltpu.make_async_copy(got2, got2, r2).wait()
    back = got2[...].astype(F32).reshape(ROWS, 2, 8, NG)
    back = jnp.concatenate(
        [back[:, 0].reshape(256, NG), back[:, 1].reshape(256, NG)], axis=1).astype(BF)
    back = dot(depth_forward, back).astype(BF)
    back = jnp.concatenate(
        [
            jnp.concatenate(
                [back[p * NG + u * 64:p * NG + u * 64 + 64, s * NG:(s + 1) * NG] for u in range(2)],
                axis=1)
            for s in range(2) for p in range(2)
        ], axis=0)
    for c in range(8):
        at = slice(c * 512, (c + 1) * 512)
        u = dot(back, stick_hot[:, at])
        hit = lax.broadcasted_iota(jnp.int32, (64, 512), 0) == cells[:, at] // NG % 64
        kin = kinetic[:, at]
        for s in range(2):
            v = jnp.concatenate(
                [jnp.sum(jnp.where(hit, u[(2 * s + p) * 64:(2 * s + p + 1) * 64], 0.0),
                         axis=0, keepdims=True) for p in range(2)], axis=0)
            applied[s, :, at] = v + kin * trial[s, :, at]

    for c in range(CH):
        z_copy(c).wait_recv()
        total = own_part[c] + part_in[c].astype(F32)
        rotated[:, :, c * width:(c + 1) * width] = total.astype(BF).reshape(16, 2, width)

    pltpu.make_async_copy(all_columns.at[pl.ds(0, ROWS - 1)], all_columns.at[pl.ds(0, ROWS - 1)], col_send).wait()
    for sem in (s1, s2):
        pltpu.make_async_copy(got2.at[pl.ds(0, ROWS - 1)], got2.at[pl.ds(0, ROWS - 1)], sem).wait()
    for c in range(CH):
        for d in range(1, XS):
            x_copy(c, d).wait_send()
        z_copy(c).wait_send()


def local(trial, resident, potential, columns, cells, slab, owner, rotation):
    npw = cells.shape[0]
    width = npw // CH
    vmem = pl.BlockSpec(memory_space=pltpu.VMEM)
    smem = pl.BlockSpec(memory_space=pltpu.SMEM)
    dma = pltpu.SemaphoreType.DMA
    return pl.pallas_call(
        kernel,
        out_shape=(
            jax.ShapeDtypeStruct(trial.shape, F32),
            jax.ShapeDtypeStruct(resident.shape, BF),
        ),
        in_specs=[vmem, vmem, vmem, vmem, vmem, smem, smem, vmem, vmem],
        out_specs=(vmem, vmem),
        scratch_shapes=[
            pltpu.VMEM((ROWS, 1, NG), jnp.int32),
            pltpu.VMEM((256, npw), BF),
            pltpu.VMEM((256, ROWS * NG), BF),
            pltpu.VMEM((1, npw), F32),
            pltpu.VMEM((ROWS, 16, NG), BF),
            pltpu.VMEM((ROWS, 16, NG), BF),
            pltpu.VMEM((ROWS, 16, NG), BF),
            pltpu.VMEM((ROWS, 16, NG), BF),
            pltpu.VMEM((1024, 256), F32),
            pltpu.VMEM((1024, 256), BF),
            pltpu.VMEM((CH, XS, 32, width), BF),
            pltpu.VMEM((CH, 32, width), F32),
            pltpu.VMEM((CH, 32, width), BF),
            pltpu.VMEM((CH, 32, width), BF),
            pltpu.VMEM((32, NG), BF),
            pltpu.VMEM((32, NG), BF),
            dma, dma, dma, dma((GR,)), dma, dma,
            dma((CH, XS - 1)), dma((CH, XS - 1)), dma((CH,)), dma((CH,)), dma, dma,
        ],
        compiler_params=pltpu.CompilerParams(
            collective_id=0, has_side_effects=True, vmem_limit_bytes=48 * 2**20
        ),
        cost_estimate=pl.CostEstimate(
            flops=4 * 10**9, bytes_accessed=2 * 10**6, transcendentals=0
        ),
    )(
        trial, resident, potential, columns.reshape(1, NG), cells.reshape(1, npw),
        slab, owner, rotation.T, tables(),
    )


def solution(mesh):
    return jax.shard_map(
        local,
        mesh=mesh,
        in_specs=(
            P("col", None, "row"), P("col", None, "row"), P("row", None, None),
            P("row"), P("row"), P(), P(), P(None, "col"),
        ),
        out_specs=(P("col", None, "row"), P("col", None, "row")),
        check_vma=False,
    )
```

profile of v0, /device:TPU:57, one launch (start us, length us, event | category | flops | bytes accessed | tf_op | source)
XLA Modules:
  0.0 45.3 jit_solution(8913183601839918766)
XLA Ops:
  0.6 0.0 copy-start.4
  0.6 0.0 copy-start.5
  0.7 0.0 copy-start.6
  0.7 0.0 copy-start.7
  0.7 0.6 %copy-done.4 = bf16[128,16]{0,1:T(8,128)(2,1)S(1)} copy-done((bf16[128,16]{0,1:T(8,128)(2,1)S(1)}, bf16[128,16]{0,1:T(8,128)(2,1)}, u32[]{:S(2)}) %copy-start.4) | copy-done | bytes 4120
  1.3 0.0 copy-done.5
  1.3 0.0 copy-done.6
  1.3 0.0 copy-done.7
  1.3 0.0 copy-start
  1.3 0.9 %copy-done = bf16[16,2,4096]{2,1,0:T(2,128)(2,1)S(1)} copy-done((bf16[16,2,4096]{2,1,0:T(2,128)(2,1)S(1)}, bf16[16,2,4096]{2,1,0:T(2,128)(2,1)}, u32[]{:S(2)}) %copy-start) | copy-done | bytes 262168
  2.3 0.0 copy-start.1
  2.3 0.9 %copy-done.1 = f32[4,128,128]{2,1,0:T(8,128)S(1)} copy-done((f32[4,128,128]{2,1,0:T(8,128)S(1)}, f32[4,128,128]{2,1,0:T(8,128)}, u32[]{:S(2)}) %copy-start.1) | copy-done | bytes 262168
  3.2 0.0 copy-start.2
  3.2 0.8 %copy-done.2 = f32[2,2,4096]{2,1,0:T(2,128)S(1)} copy-done((f32[2,2,4096]{2,1,0:T(2,128)S(1)}, f32[2,2,4096]{2,1,0:T(2,128)}, u32[]{:S(2)}) %copy-start.2) | copy-done | bytes 65560
  4.1 0.0 copy-start.3
  4.1 0.7 %copy-done.3 = s32[4096]{0:T(1024)S(1)} copy-done((s32[4096]{0:T(1024)S(1)}, s32[4096]{0:T(1024)}, u32[]{:S(2)}) %copy-start.3) | copy-done | bytes 16408
  4.8 0.0 copy-start.8
  4.8 0.9 %copy-done.8 = bf16[2,256,256]{2,1,0:T(8,128)(2,1)S(1)} copy-done((bf16[2,256,256]{2,1,0:T(8,128)(2,1)S(1)}, bf16[2,256,256]{2,1,0:T(8,128)(2,1)}, u32[]{:S(2)}) %copy-start.8) | copy-done | bytes 262168
  5.7 38.2 %shard_map.104 = (f32[2,2,4096]{2,1,0:T(2,128)S(1)}, bf16[16,2,4096]{2,1,0:T(2,128)(2,1)S(1)}) custom-call(f32[2,2,4096]{2,1,0:T(2,128)S(1)} %copy-done.2, bf16[16,2,4096]{2,1,0:T(2,128)(2,1)S(1)} %copy-done, f32[4,128,128]{2,1,0:T(8,128)S(1)} %copy-done.1, s32[1,128]{1,0:T(1,128)S(1)} %bitcast.5, s32[1,4096]{1,0:T(1,128)S(1)} %bitcast.3, s32[32]{0:T(128)S(1)} %copy-done.6, ...), custom_call_target="tpu_custom_call" | custom-call | flops 4000000000 | bytes 2000000 | tf_op jit(solution)/shard_map/pallas_call | solution.py:325
  43.9 0.6 %copy.13 = f32[2,2,4096]{2,1,0:T(2,128)} copy(f32[2,2,4096]{2,1,0:T(2,128)S(1)} %get-tuple-element.4) | data formatting | bytes 131072
  44.6 0.7 %copy.14 = bf16[16,2,4096]{2,1,0:T(2,128)(2,1)} copy(bf16[16,2,4096]{2,1,0:T(2,128)(2,1)S(1)} %get-tuple-element.5) | data formatting | bytes 524288
Async XLA Ops:
  0.6 0.7 %copy-start.4 = (bf16[128,16]{0,1:T(8,128)(2,1)S(1)}, bf16[128,16]{0,1:T(8,128)(2,1)}, u32[]{:S(2)}) copy-start(bf16[128,16]{0,1:T(8,128)(2,1)} %param.16) | copy-start | bytes 12292
  0.6 0.7 %copy-start.5 = (s32[128]{0:T(128)S(1)}, s32[128]{0:T(128)}, u32[]{:S(2)}) copy-start(s32[128]{0:T(128)} %param.12) | copy-start | bytes 1540
  0.7 0.7 %copy-start.6 = (s32[32]{0:T(128)S(1)}, s32[32]{0:T(128)}, u32[]{:S(2)}) copy-start(s32[32]{0:T(128)} %slab.1) | copy-start | bytes 388
  0.7 0.7 %copy-start.7 = (s32[8]{0:T(128)S(1)}, s32[8]{0:T(128)}, u32[]{:S(2)}) copy-start(s32[8]{0:T(128)} %owner.1) | copy-start | bytes 100
  1.3 0.9 %copy-start = (bf16[16,2,4096]{2,1,0:T(2,128)(2,1)S(1)}, bf16[16,2,4096]{2,1,0:T(2,128)(2,1)}, u32[]{:S(2)}) copy-start(bf16[16,2,4096]{2,1,0:T(2,128)(2,1)} %resident.1) | copy-start | bytes 786436
  2.3 0.9 %copy-start.1 = (f32[4,128,128]{2,1,0:T(8,128)S(1)}, f32[4,128,128]{2,1,0:T(8,128)}, u32[]{:S(2)}) copy-start(f32[4,128,128]{2,1,0:T(8,128)} %potential.1) | copy-start | bytes 786436
  3.2 0.8 %copy-start.2 = (f32[2,2,4096]{2,1,0:T(2,128)S(1)}, f32[2,2,4096]{2,1,0:T(2,128)}, u32[]{:S(2)}) copy-start(f32[2,2,4096]{2,1,0:T(2,128)} %trial.1) | copy-start | bytes 196612
  4.1 0.7 %copy-start.3 = (s32[4096]{0:T(1024)S(1)}, s32[4096]{0:T(1024)}, u32[]{:S(2)}) copy-start(s32[4096]{0:T(1024)} %param.13) | copy-start | bytes 49156
  4.8 0.9 %copy-start.8 = (bf16[2,256,256]{2,1,0:T(8,128)(2,1)S(1)}, bf16[2,256,256]{2,1,0:T(8,128)(2,1)}, u32[]{:S(2)}) copy-start(bf16[2,256,256]{2,1,0:T(8,128)(2,1)} %constant.2.clone.table) | copy-start | bytes 786436
where the time goes:
time: 45.6 us; the launch traced here: 45.3 us
  Pallas kernels  38.2 us (84%)
  local copies, waits for them, and re-layouts  6.41 us (14%)
  between operations  0.68 us (1%)
    pallas_call x1, Pallas kernels, local(): pl.pallas_call(kernel, out_shape=(jax.ShapeDtypeStruct(trial.shape, F32),...  38.2 us
    unnamed x20, local copies, waits for them, and re-layouts  6.41 us

commit v1 on v0

--- a/solution.py
+++ b/solution.py
@@ -9,7 +9,10 @@
 NG = 128
 ROWS = 32
 XS = 4
-CH = 4
+PAIRS = ROWS // 2
+CH = 8
+EARLY = 4
+PLAN = {"start": (0,), "fill1": (1,), "fill3": (2,), "plane0": (3,), "plane1": (4,), "pick7": (5,), "pick15": (6,), "end": (7,)}
 GR = 4
 MESH = pl.DeviceIdType.MESH
 F32 = jnp.float32
@@ -34,16 +37,26 @@
     return jnp.where(j < NG // 2, j, j - NG).astype(F32)
 
 
-def tables():
-    phase = 2.0 * np.pi / NG * (np.outer(np.arange(NG), np.arange(NG)) % NG)
-    c, s = np.cos(phase), np.sin(phase)
-    base = np.block([[c, -s], [s, c]])
-    return jnp.asarray(np.stack([base, base.T]), BF)
+def make_table(table):
+    a = lax.broadcasted_iota(jnp.int32, (NG, NG), 0)
+    b = lax.broadcasted_iota(jnp.int32, (NG, NG), 1)
+    step = lax.broadcasted_iota(jnp.int32, (8, NG), 1).astype(F32)
+    wave = jnp.tile(jnp.cos(step * (2.0 * np.pi / NG)), (NG // 8, 1))
+    k = a * b
+    c = jnp.take_along_axis(wave, k % NG, axis=1)
+    s = jnp.take_along_axis(wave, (k + 3 * NG // 4) % NG, axis=1)
+    top = jnp.concatenate([c, -s], axis=1)
+    flip = jnp.concatenate([c, s], axis=1)
+    low = jnp.concatenate([s, c], axis=1)
+    table[0] = jnp.concatenate([top, low], axis=0).astype(BF)
+    low = jnp.concatenate([-s, c], axis=1)
+    table[1] = jnp.concatenate([flip, low], axis=0).astype(BF)
 
 
 def kernel(
-    trial, resident, potential, columns, cells, slab, owner, rotation, table,
+    trial_in, resident_in, potential_in, columns_in, cells_in, slab_in, owner_in, rotation_in,
     applied, rotated,
+    trial, resident, potential, columns, cells, slab, owner, rotation, table, loads,
     all_columns, stick_hot, plane_hot, kinetic, sent1, got1, sent2, got2,
     grid, picked, panels, own_part, part_out, part_in, weight_out, weight_in,
     col_send, col_recv, s1, r1, s2, r2, xs, xr, zs, zr, ws, wr,
@@ -53,11 +66,31 @@
     half = col // XS
     x = lax.rem(col, XS)
     mate = lax.rem(col + XS, 2 * XS)
-    npw = cells.shape[-1]
+    pair = row // 2
+    core = lax.rem(row, 2)
+    sibling = row + 1 - 2 * core
+    npw = cells_in.shape[-1]
     width = npw // CH
 
     def x_peer(d):
         return half * XS + lax.rem(x + d, XS)
+
+    def peer(q, i):
+        return lax.rem(pair + q, PAIRS) * 2 + i
+
+    def slot(q):
+        return lax.rem(PAIRS - q, PAIRS) * 2 + core
+
+    load = [
+        pltpu.make_async_copy(source, target, loads.at[i])
+        for i, (source, target) in enumerate((
+            (columns_in, columns), (cells_in, cells), (resident_in, resident),
+            (rotation_in, rotation), (trial_in, trial), (potential_in, potential),
+            (slab_in, slab), (owner_in, owner),
+        ))
+    ]
+    for i in (1, 4, 2, 0, 6, 3, 7, 5):
+        load[i].start()
 
     barrier = pltpu.get_barrier_semaphore()
 
@@ -72,10 +105,114 @@
         pl.semaphore_signal(barrier, inc=1, device_id=(x_peer(d), row), device_id_type=MESH)
     pl.semaphore_signal(barrier, inc=1, device_id=(mate, row), device_id_type=MESH)
 
+    make_table(table)
+
+    load[1].wait()
+    load[4].wait()
+
+    def stick_part(c):
+        at = slice(c * 512, (c + 1) * 512)
+        cell = cells[:, at]
+        z = cell // NG
+        hot = onehot((z // 64) * NG + cell % NG, 256)
+        stick_hot[:, at] = hot
+        hit = lax.broadcasted_iota(jnp.int32, (64, 512), 0) == z % 64
+        left = jnp.concatenate(
+            [jnp.where(hit, trial[s, p:p + 1, at], 0.0) for s in range(2) for p in range(2)],
+            axis=0,
+        ).astype(BF)
+        return dot_nt(left, hot)
+
+    def sticks(first, last, acc=None):
+        for c in range(first, last):
+            acc = stick_part(c) if acc is None else acc + stick_part(c)
+        return acc
+
+    filled = sticks(0, EARLY) if EARLY else None
+
+    load[2].wait()
     for c in range(CH):
         block = resident[:, :, c * width:(c + 1) * width].reshape(32, width)
         panels[c, pl.ds(x, 1)] = block[None]
-
+    load[0].wait()
+    all_columns[pl.ds(core, 1)] = columns[...].reshape(1, 1, NG)
+
+    pl.semaphore_wait(barrier, ROWS - 1 + XS - 1 + 1)
+
+    def x_copy(c, d):
+        return pltpu.make_async_remote_copy(
+            panels.at[c, x], panels.at[c, x], xs.at[c, d - 1], xr.at[c, d - 1],
+            device_id=(x_peer(d), row), device_id_type=MESH,
+        )
+
+    def x_arrival(c, d):
+        return pltpu.make_async_remote_copy(
+            panels.at[c, x], panels.at[c, lax.rem(x + XS - d, XS)], xs.at[c, d - 1], xr.at[c, d - 1],
+            device_id=(x_peer(d), row), device_id_type=MESH,
+        )
+
+    def send_column(q, i, to):
+        pltpu.make_async_remote_copy(
+            columns, all_columns.at[slot(q)], col_send, col_recv,
+            device_id=(col, to), device_id_type=MESH,
+        ).start()
+
+    for d in (2, 1, 3):
+        x_copy(0, d).start()
+    send_column(0, 0, sibling)
+
+    def send_columns(q, carry):
+        send_column(q, 0, peer(q, 0))
+        send_column(q, 1, peer(q, 1))
+        return carry
+
+    lax.fori_loop(1, PAIRS, send_columns, 0)
+    for c in range(1, CH):
+        for d in (2, 1, 3):
+            x_copy(c, d).start()
+
+    filled = sticks(EARLY, 8, filled)
+    filled = jnp.concatenate(
+        [
+            jnp.concatenate(
+                [filled[(2 * s + p) * 64:(2 * s + p + 1) * 64, u * NG:(u + 1) * NG]
+                 for p in range(2) for u in range(2)], axis=0)
+            for s in range(2)
+        ], axis=1).astype(BF)
+
+    load[6].wait()
+    j = lax.broadcasted_iota(jnp.int32, (8, 256), 0)
+    k = lax.broadcasted_iota(jnp.int32, (8, 256), 1)
+    want = j // 4 * NG + j % 4
+    order = jnp.concatenate(
+        [jnp.where(k == want + slab[r] * 4, 1.0, 0.0) for r in range(ROWS)], axis=0
+    ).astype(BF)
+    depth_inverse = dot(order, table[0]).astype(BF)
+    spread_z = dot(depth_inverse, filled)
+    for r in range(ROWS):
+        rows = slice(8 * r, 8 * r + 8)
+        sent1[r] = jnp.concatenate([spread_z[rows, :NG], spread_z[rows, NG:]], axis=0).astype(BF)
+
+    def send_stick(q, to):
+        at = slot(q)
+        pltpu.make_async_remote_copy(
+            sent1.at[to], got1.at[at], s1, r1.at[at // (ROWS // GR)],
+            device_id=(col, to), device_id_type=MESH,
+        ).start()
+
+    send_stick(0, sibling)
+
+    def send_sticks(n, carry):
+        q = PAIRS - n
+        send_stick(q, peer(q, 0))
+        send_stick(q, peer(q, 1))
+        return carry
+
+    lax.fori_loop(1, PAIRS, send_sticks, 0)
+    pltpu.make_async_copy(sent1.at[row], got1.at[core], r1.at[0]).start()
+
+    load[3].wait()
+    load[7].wait()
     lane = lax.broadcasted_iota(jnp.int32, (16, NG), 1)
     sub = lax.broadcasted_iota(jnp.int32, (16, NG), 0)
     perm = jnp.concatenate(
@@ -96,100 +233,10 @@
     spread = jnp.where(same, spread, 0.0)
     weight_own = jnp.where(half == 0, spread[:, :NG], spread[:, NG:]).astype(BF)
     weight_out[...] = jnp.where(half == 0, spread[:, NG:], spread[:, :NG]).astype(BF)
-    all_columns[pl.ds(row, 1)] = columns[...].reshape(1, 1, NG)
-
-    for c in range(8):
-        cell = cells[:, c * 512:(c + 1) * 512]
-        z = cell // NG
-        stick_hot[:, c * 512:(c + 1) * 512] = onehot((z // 64) * NG + cell % NG, 256)
-
-    pl.semaphore_wait(barrier, ROWS - 1 + XS - 1 + 1)
-
-    def send_columns(d, carry):
-        pltpu.make_async_remote_copy(
-            columns, all_columns.at[row], col_send, col_recv,
-            device_id=(col, lax.rem(row + d, ROWS)), device_id_type=MESH,
-        ).start()
-        return carry
-
-    lax.fori_loop(1, ROWS, send_columns, 0)
     w_copy = pltpu.make_async_remote_copy(
         weight_out, weight_in, ws, wr, device_id=(mate, row), device_id_type=MESH
     )
     w_copy.start()
-
-    def x_copy(c, d):
-        return pltpu.make_async_remote_copy(
-            panels.at[c, x], panels.at[c, x], xs.at[c, d - 1], xr.at[c, d - 1],
-            device_id=(x_peer(d), row), device_id_type=MESH,
-        )
-
-    def x_arrival(c, d):
-        return pltpu.make_async_remote_copy(
-            panels.at[c, x], panels.at[c, lax.rem(x + XS - d, XS)], xs.at[c, d - 1], xr.at[c, d - 1],
-            device_id=(x_peer(d), row), device_id_type=MESH,
-        )
-
-    for c in range(CH):
-        for d in (2, 1, 3):
-            x_copy(c, d).start()
-
-    def stick_part(c, acc):
-        at = pl.ds(pl.multiple_of(c * 512, 512), 512)
-        zh = cells[:, at] // NG % 64
-        hit = lax.broadcasted_iota(jnp.int32, (64, 512), 0) == zh
-        left = jnp.concatenate(
-            [jnp.where(hit, trial[s, p:p + 1, at], 0.0) for s in range(2) for p in range(2)],
-            axis=0,
-        ).astype(BF)
-        return acc + dot_nt(left, stick_hot[:, at])
-
-    filled = lax.fori_loop(0, 8, stick_part, jnp.zeros((256, 256), F32))
-    filled = jnp.concatenate(
-        [
-            jnp.concatenate(
-                [filled[(2 * s + p) * 64:(2 * s + p + 1) * 64, u * NG:(u + 1) * NG]
-                 for p in range(2) for u in range(2)], axis=0)
-            for s in range(2)
-        ], axis=1).astype(BF)
-
-    j = lax.broadcasted_iota(jnp.int32, (8, 256), 0)
-    k = lax.broadcasted_iota(jnp.int32, (8, 256), 1)
-    want = j // 4 * NG + j % 4
-    order = jnp.concatenate(
-        [jnp.where(k == want + slab[r] * 4, 1.0, 0.0) for r in range(ROWS)], axis=0
-    ).astype(BF)
-    depth_inverse = dot(order, table[0]).astype(BF)
-    depth_forward = dot_nt(table[1], order).astype(BF)
-    spread_z = dot(depth_inverse, filled)
-    for r in range(ROWS):
-        rows = slice(8 * r, 8 * r + 8)
-        sent1[r] = jnp.concatenate([spread_z[rows, :NG], spread_z[rows, NG:]], axis=0).astype(BF)
-
-    def exchange(source, target, send_sem, recv_sem):
-        def go(d, carry):
-            to = lax.rem(row + d, ROWS)
-            pltpu.make_async_remote_copy(
-                source.at[to], target.at[row], send_sem, recv_sem,
-                device_id=(col, to), device_id_type=MESH,
-            ).start()
-            return carry
-
-        lax.fori_loop(1, ROWS, go, 0)
-        pltpu.make_async_copy(source.at[row], target.at[row], recv_sem).start()
-
-    exchange(sent1, got1, s1, r1.at[row // (ROWS // GR)])
-
-    own_col = columns[...]
-    fx, fy = frequency(own_col // NG), frequency(own_col % NG)
-    rows16 = lax.broadcasted_iota(jnp.int32, (16, NG), 0)
-    fxy = jnp.where(rows16 == 0, fx, jnp.where(rows16 == 1, fy, 0.0))
-    fxy = jnp.concatenate([fxy, fxy], axis=1).astype(BF)
-    for c in range(8):
-        at = slice(c * 512, (c + 1) * 512)
-        f = dot(fxy, stick_hot[:, at])
-        fz = frequency(cells[:, at] // NG)
-        kinetic[:, at] = 2.0 * (f[0:1] * f[0:1] + f[1:2] * f[1:2] + fz * fz) / (NG * NG)
 
     pltpu.make_async_copy(all_columns.at[pl.ds(0, ROWS - 1)], all_columns.at[pl.ds(0, ROWS - 1)], col_recv).wait()
     for c in range(8):
@@ -212,6 +259,12 @@
             part_out.at[c], part_in.at[c], zs.at[c], zr.at[c],
             device_id=(mate, row), device_id_type=MESH,
         )
+
+    def rotations(place):
+        for c in PLAN.get(place, ()):
+            rotate(c)
+
+    rotations("start")
 
     per = ROWS // GR
     for g in range(GR):
@@ -229,9 +282,9 @@
                 grid[256 * m:256 * m + 256] = part
             else:
                 grid[256 * m:256 * m + 256] += part
-
-    rotate(0)
-    forward_x, forward_y = table[0], table[1]
+        rotations("fill%d" % g)
+
+    load[5].wait()
     for s in range(2):
         for q in range(4):
             cp = [(s * 2 + p) * 4 + q for p in range(2)]
@@ -249,35 +302,37 @@
             for p in range(2):
                 picked[cp[p] * 64:(cp[p] + 1) * 64] = jnp.concatenate(
                     [t[p * NG:p * NG + 64], t[p * NG + 64:p * NG + NG]], axis=1)
-
-    rotate(1)
-
-    def pick(n, carry):
-        pair = lax.rem(row // 2 + n, ROWS // 2)
-        at = pl.ds(pl.multiple_of(pair * 256, 256), 256)
-        u = dot(picked[...], plane_hot[:, at])
-        key = jnp.concatenate([all_columns[2 * pair], all_columns[2 * pair + 1]], axis=1)
+        rotations("plane%d" % s)
+
+    for q in range(PAIRS):
+        u = dot(picked[...], plane_hot[:, q * 256:q * 256 + 256])
+        key = jnp.concatenate([all_columns[2 * q], all_columns[2 * q + 1]], axis=1)
         hit = lax.broadcasted_iota(jnp.int32, (64, 256), 0) == key // NG % 64
         got = jnp.concatenate(
             [jnp.sum(jnp.where(hit, u[i * 64:(i + 1) * 64], 0.0), axis=0, keepdims=True)
              for i in range(16)], axis=0).astype(BF)
         for i in range(2):
-            to = 2 * pair + i
-            sent2[to] = got[:, i * NG:(i + 1) * NG]
-
-            @pl.when(to != row)
-            def _():
-                pltpu.make_async_remote_copy(
-                    sent2.at[to], got2.at[row], s2, r2,
-                    device_id=(col, to), device_id_type=MESH,
-                ).start()
-
-        return carry
-
-    lax.fori_loop(0, ROWS // 2, pick, 0)
-    pltpu.make_async_copy(sent2.at[row], got2.at[row], r2).start()
-    rotate(2)
-    rotate(3)
+            sent2[2 * q + i] = got[:, i * NG:(i + 1) * NG]
+        for i in range(2) if q else (0,):
+            pltpu.make_async_remote_copy(
+                sent2.at[2 * q + i] if q else sent2.at[1 - core], got2.at[row], s2, r2,
+                device_id=(col, peer(q, i) if q else sibling), device_id_type=MESH,
+            ).start()
+        rotations("pick%d" % q)
+    pltpu.make_async_copy(sent2.at[core], got2.at[row], r2).start()
+
+    own_col = columns[...]
+    fx, fy = frequency(own_col // NG), frequency(own_col % NG)
+    rows16 = lax.broadcasted_iota(jnp.int32, (16, NG), 0)
+    fxy = jnp.where(rows16 == 0, fx, jnp.where(rows16 == 1, fy, 0.0))
+    fxy = jnp.concatenate([fxy, fxy], axis=1).astype(BF)
+    for c in range(8):
+        at = slice(c * 512, (c + 1) * 512)
+        f = dot(fxy, stick_hot[:, at])
+        fz = frequency(cells[:, at] // NG)
+        kinetic[:, at] = 2.0 * (f[0:1] * f[0:1] + f[1:2] * f[1:2] + fz * fz) / (NG * NG)
+    depth_forward = dot_nt(table[1], order).astype(BF)
+    rotations("end")
 
     pltpu.make_async_copy(got2, got2, r2).wait()
     back = got2[...].astype(F32).reshape(ROWS, 2, 8, NG)
@@ -320,17 +375,27 @@
     npw = cells.shape[0]
     width = npw // CH
     vmem = pl.BlockSpec(memory_space=pltpu.VMEM)
-    smem = pl.BlockSpec(memory_space=pltpu.SMEM)
+    hbm = pl.BlockSpec(memory_space=pl.ANY)
     dma = pltpu.SemaphoreType.DMA
     return pl.pallas_call(
         kernel,
         out_shape=(
-            jax.ShapeDtypeStruct(trial.shape, F32),
-            jax.ShapeDtypeStruct(resident.shape, BF),
+            pltpu.VMEM(trial.shape, F32),
+            pltpu.VMEM(resident.shape, BF),
         ),
-        in_specs=[vmem, vmem, vmem, vmem, vmem, smem, smem, vmem, vmem],
+        in_specs=[hbm] * 8,
         out_specs=(vmem, vmem),
         scratch_shapes=[
+            pltpu.VMEM(trial.shape, F32),
+            pltpu.VMEM(resident.shape, BF),
+            pltpu.VMEM(potential.shape, F32),
+            pltpu.VMEM((1, NG), jnp.int32),
+            pltpu.VMEM((1, npw), jnp.int32),
+            pltpu.SMEM((ROWS,), jnp.int32),
+            pltpu.SMEM((8,), jnp.int32),
+            pltpu.VMEM((16, NG), BF),
+            pltpu.VMEM((2, 256, 256), BF),
+            dma((8,)),
             pltpu.VMEM((ROWS, 1, NG), jnp.int32),
             pltpu.VMEM((256, npw), BF),
             pltpu.VMEM((256, ROWS * NG), BF),
@@ -356,10 +421,13 @@
         cost_estimate=pl.CostEstimate(
             flops=4 * 10**9, bytes_accessed=2 * 10**6, transcendentals=0
         ),
-    )(
-        trial, resident, potential, columns.reshape(1, NG), cells.reshape(1, npw),
-        slab, owner, rotation.T, tables(),
-    )
+    )(*(
+        pltpu.with_memory_space_constraint(operand, pltpu.HBM)
+        for operand in (
+            trial, resident, potential, columns.reshape(1, NG), cells.reshape(1, npw),
+            slab, owner, rotation.T,
+        )
+    ))
 
 
 def solution(mesh):

time: 45.6 us -> 40.9 us (0.90)
  the two profiles are of different devices: /device:TPU:57 before, /device:TPU:1 now
where the time goes in v1:
time: 40.9 us; the launch traced here: 40.7 us
  Pallas kernels  38.7 us (95%)
  local copies, waits for them, and re-layouts  1.33 us (3%)
  between operations  0.64 us (2%)
    pallas_call x1, Pallas kernels, local(): pl.pallas_call(kernel, out_shape=(pltpu.VMEM(trial.shape, F32), pltpu.VME...  38.7 us
    unnamed x2, local copies, waits for them, and re-layouts  1.33 us

profile of v1, /device:TPU:1, one launch (start us, length us, event | category | flops | bytes accessed | tf_op | source)
XLA Modules:
  0.0 40.7 jit_solution(9574931737522761187)
XLA Ops:
  0.6 38.7 %shard_map.95 = (f32[2,2,4096]{2,1,0:T(2,128)S(1)}, bf16[16,2,4096]{2,1,0:T(2,128)(2,1)S(1)}) custom-call(f32[2,2,4096]{2,1,0:T(2,128)} %trial_in.1, bf16[16,2,4096]{2,1,0:T(2,128)(2,1)} %resident_in.1, f32[4,128,128]{2,1,0:T(8,128)} %potential_in.1, s32[1,128]{1,0:T(1,128)} %bitcast.5, s32[1,4096]{1,0:T(1,128)} %bitcast.3, s32[32]{0:T(128)} %slab_in.1, ...), custom_call_target="tpu_custom_call" | custom-call | flops 4000000000 | bytes 2000000 | tf_op jit(solution)/shard_map/pallas_call | solution.py:380
  39.4 0.6 %copy.12 = f32[2,2,4096]{2,1,0:T(2,128)} copy(f32[2,2,4096]{2,1,0:T(2,128)S(1)} %get-tuple-element.2) | data formatting | bytes 131072
  40.0 0.7 %copy.13 = bf16[16,2,4096]{2,1,0:T(2,128)(2,1)} copy(bf16[16,2,4096]{2,1,0:T(2,128)(2,1)S(1)} %get-tuple-element.3) | data formatting | bytes 524288

commit v2 on v1

--- a/solution.py
+++ b/solution.py
@@ -11,8 +11,9 @@
 XS = 4
 PAIRS = ROWS // 2
 CH = 8
-EARLY = 4
-PLAN = {"start": (0,), "fill1": (1,), "fill3": (2,), "plane0": (3,), "plane1": (4,), "pick7": (5,), "pick15": (6,), "end": (7,)}
+EARLY = 0
+LATE = 2
+PLAN = {"sent": (0,), "start": (1,), "fill1": (2,), "fill3": (3,), "plane0": (4,), "plane1": (5,), "pick5": (6,), "pick10": (7,)}
 GR = 4
 MESH = pl.DeviceIdType.MESH
 F32 = jnp.float32
@@ -136,80 +137,6 @@
         panels[c, pl.ds(x, 1)] = block[None]
     load[0].wait()
     all_columns[pl.ds(core, 1)] = columns[...].reshape(1, 1, NG)
-
-    pl.semaphore_wait(barrier, ROWS - 1 + XS - 1 + 1)
-
-    def x_copy(c, d):
-        return pltpu.make_async_remote_copy(
-            panels.at[c, x], panels.at[c, x], xs.at[c, d - 1], xr.at[c, d - 1],
-            device_id=(x_peer(d), row), device_id_type=MESH,
-        )
-
-    def x_arrival(c, d):
-        return pltpu.make_async_remote_copy(
-            panels.at[c, x], panels.at[c, lax.rem(x + XS - d, XS)], xs.at[c, d - 1], xr.at[c, d - 1],
-            device_id=(x_peer(d), row), device_id_type=MESH,
-        )
-
-    def send_column(q, i, to):
-        pltpu.make_async_remote_copy(
-            columns, all_columns.at[slot(q)], col_send, col_recv,
-            device_id=(col, to), device_id_type=MESH,
-        ).start()
-
-    for d in (2, 1, 3):
-        x_copy(0, d).start()
-    send_column(0, 0, sibling)
-
-    def send_columns(q, carry):
-        send_column(q, 0, peer(q, 0))
-        send_column(q, 1, peer(q, 1))
-        return carry
-
-    lax.fori_loop(1, PAIRS, send_columns, 0)
-    for c in range(1, CH):
-        for d in (2, 1, 3):
-            x_copy(c, d).start()
-
-    filled = sticks(EARLY, 8, filled)
-    filled = jnp.concatenate(
-        [
-            jnp.concatenate(
-                [filled[(2 * s + p) * 64:(2 * s + p + 1) * 64, u * NG:(u + 1) * NG]
-                 for p in range(2) for u in range(2)], axis=0)
-            for s in range(2)
-        ], axis=1).astype(BF)
-
-    load[6].wait()
-    j = lax.broadcasted_iota(jnp.int32, (8, 256), 0)
-    k = lax.broadcasted_iota(jnp.int32, (8, 256), 1)
-    want = j // 4 * NG + j % 4
-    order = jnp.concatenate(
-        [jnp.where(k == want + slab[r] * 4, 1.0, 0.0) for r in range(ROWS)], axis=0
-    ).astype(BF)
-    depth_inverse = dot(order, table[0]).astype(BF)
-    spread_z = dot(depth_inverse, filled)
-    for r in range(ROWS):
-        rows = slice(8 * r, 8 * r + 8)
-        sent1[r] = jnp.concatenate([spread_z[rows, :NG], spread_z[rows, NG:]], axis=0).astype(BF)
-
-    def send_stick(q, to):
-        at = slot(q)
-        pltpu.make_async_remote_copy(
-            sent1.at[to], got1.at[at], s1, r1.at[at // (ROWS // GR)],
-            device_id=(col, to), device_id_type=MESH,
-        ).start()
-
-    send_stick(0, sibling)
-
-    def send_sticks(n, carry):
-        q = PAIRS - n
-        send_stick(q, peer(q, 0))
-        send_stick(q, peer(q, 1))
-        return carry
-
-    lax.fori_loop(1, PAIRS, send_sticks, 0)
-    pltpu.make_async_copy(sent1.at[row], got1.at[core], r1.at[0]).start()
 
     load[3].wait()
     load[7].wait()
@@ -233,15 +160,24 @@
     spread = jnp.where(same, spread, 0.0)
     weight_own = jnp.where(half == 0, spread[:, :NG], spread[:, NG:]).astype(BF)
     weight_out[...] = jnp.where(half == 0, spread[:, NG:], spread[:, :NG]).astype(BF)
+    pl.semaphore_wait(barrier, ROWS - 1 + XS - 1 + 1)
+
     w_copy = pltpu.make_async_remote_copy(
         weight_out, weight_in, ws, wr, device_id=(mate, row), device_id_type=MESH
     )
     w_copy.start()
 
-    pltpu.make_async_copy(all_columns.at[pl.ds(0, ROWS - 1)], all_columns.at[pl.ds(0, ROWS - 1)], col_recv).wait()
-    for c in range(8):
-        key = jnp.concatenate([all_columns[4 * c + i] for i in range(4)], axis=1)
-        plane_hot[:, c * 512:(c + 1) * 512] = onehot(key // (64 * NG) * NG + key % NG, 256)
+    def x_copy(c, d):
+        return pltpu.make_async_remote_copy(
+            panels.at[c, x], panels.at[c, x], xs.at[c, d - 1], xr.at[c, d - 1],
+            device_id=(x_peer(d), row), device_id_type=MESH,
+        )
+
+    def x_arrival(c, d):
+        return pltpu.make_async_remote_copy(
+            panels.at[c, x], panels.at[c, lax.rem(x + XS - d, XS)], xs.at[c, d - 1], xr.at[c, d - 1],
+            device_id=(x_peer(d), row), device_id_type=MESH,
+        )
 
     def rotate(c):
         if c == 0:
@@ -263,6 +199,76 @@
     def rotations(place):
         for c in PLAN.get(place, ()):
             rotate(c)
+
+    def send_column(q, i, to):
+        pltpu.make_async_remote_copy(
+            columns, all_columns.at[slot(q)], col_send, col_recv,
+            device_id=(col, to), device_id_type=MESH,
+        ).start()
+
+    for d in (2, 1, 3):
+        x_copy(0, d).start()
+    send_column(0, 0, sibling)
+
+    def send_columns(q, carry):
+        send_column(q, 0, peer(q, 0))
+        send_column(q, 1, peer(q, 1))
+        return carry
+
+    lax.fori_loop(1, PAIRS, send_columns, 0)
+    for c in range(1, LATE):
+        for d in (2, 1, 3):
+            x_copy(c, d).start()
+
+    filled = sticks(EARLY, 8, filled)
+    filled = jnp.concatenate(
+        [
+            jnp.concatenate(
+                [filled[(2 * s + p) * 64:(2 * s + p + 1) * 64, u * NG:(u + 1) * NG]
+                 for p in range(2) for u in range(2)], axis=0)
+            for s in range(2)
+        ], axis=1).astype(BF)
+
+    load[6].wait()
+    j = lax.broadcasted_iota(jnp.int32, (8, 256), 0)
+    k = lax.broadcasted_iota(jnp.int32, (8, 256), 1)
+    want = j // 4 * NG + j % 4
+    order = jnp.concatenate(
+        [jnp.where(k == want + slab[r] * 4, 1.0, 0.0) for r in range(ROWS)], axis=0
+    ).astype(BF)
+    depth_inverse = dot(order, table[0]).astype(BF)
+    spread_z = dot(depth_inverse, filled)
+    for r in range(ROWS):
+        rows = slice(8 * r, 8 * r + 8)
+        sent1[r] = jnp.concatenate([spread_z[rows, :NG], spread_z[rows, NG:]], axis=0).astype(BF)
+
+    def send_stick(q, to):
+        at = slot(q)
+        pltpu.make_async_remote_copy(
+            sent1.at[to], got1.at[at], s1, r1.at[at // (ROWS // GR)],
+            device_id=(col, to), device_id_type=MESH,
+        ).start()
+
+    send_stick(0, sibling)
+
+    def send_sticks(n, carry):
+        q = PAIRS - n
+        send_stick(q, peer(q, 0))
+        send_stick(q, peer(q, 1))
+        return carry
+
+    lax.fori_loop(1, PAIRS, send_sticks, 0)
+    pltpu.make_async_copy(sent1.at[row], got1.at[core], r1.at[0]).start()
+    for c in range(LATE, CH):
+        for d in (2, 1, 3):
+            x_copy(c, d).start()
+    rotations("sent")
+
+
+    pltpu.make_async_copy(all_columns.at[pl.ds(0, ROWS - 1)], all_columns.at[pl.ds(0, ROWS - 1)], col_recv).wait()
+    for c in range(8):
+        key = jnp.concatenate([all_columns[4 * c + i] for i in range(4)], axis=1)
+        plane_hot[:, c * 512:(c + 1) * 512] = onehot(key // (64 * NG) * NG + key % NG, 256)
 
     rotations("start")
 
@@ -285,23 +291,32 @@
         rotations("fill%d" % g)
 
     load[5].wait()
+    level = jnp.concatenate([potential[q] for q in range(4)], axis=0) * (2.0 ** -21)
+    level = jnp.concatenate([level, level], axis=1)
     for s in range(2):
+        t = jnp.concatenate(
+            [
+                jnp.concatenate(
+                    [grid[i * 64:(i + 1) * 64, u * NG:(u + 1) * NG]
+                     for i in (8 * s + q, 8 * s + 4 + q) for u in range(2)], axis=0)
+                for q in range(4)
+            ], axis=1).astype(BF)
+        t = dot(table[0], t).astype(BF)
+        t = jnp.concatenate(
+            [jnp.concatenate([t[:NG, q * NG:(q + 1) * NG], t[NG:, q * NG:(q + 1) * NG]], axis=1)
+             for q in range(4)], axis=0)
+        t = dot(t, table[1])
+        t = (t * level).astype(BF)
+        t = dot(t, table[0]).astype(BF)
+        t = jnp.concatenate(
+            [jnp.concatenate([t[q * NG:(q + 1) * NG, :NG], t[q * NG:(q + 1) * NG, NG:]], axis=0)
+             for q in range(4)], axis=1)
+        t = dot(table[1], t).astype(BF)
         for q in range(4):
-            cp = [(s * 2 + p) * 4 + q for p in range(2)]
-            block = jnp.concatenate(
-                [grid[i * 64:(i + 1) * 64, u * NG:(u + 1) * NG] for i in cp for u in range(2)],
-                axis=0).astype(BF)
-            t = dot(table[0], block)
-            t = jnp.concatenate([t[:NG], t[NG:]], axis=1).astype(BF)
-            t = dot(t, table[1])
-            v = potential[q] * (2.0 ** -21)
-            t = (t * jnp.concatenate([v, v], axis=1)).astype(BF)
-            t = dot(t, table[0])
-            t = jnp.concatenate([t[:, :NG], t[:, NG:]], axis=0).astype(BF)
-            t = dot(table[1], t).astype(BF)
             for p in range(2):
-                picked[cp[p] * 64:(cp[p] + 1) * 64] = jnp.concatenate(
-                    [t[p * NG:p * NG + 64], t[p * NG + 64:p * NG + NG]], axis=1)
+                picked[((2 * s + p) * 4 + q) * 64:((2 * s + p) * 4 + q + 1) * 64] = jnp.concatenate(
+                    [t[p * NG + u * 64:p * NG + u * 64 + 64, q * NG:(q + 1) * NG] for u in range(2)],
+                    axis=1)
         rotations("plane%d" % s)
 
     for q in range(PAIRS):

time: 40.9 us -> 38.4 us (0.939)
  Pallas kernels: 38.7 us -> 36.2 us
    pallas_call x1, Pallas kernels: 38.7 us -> 36.2 us  [local(): pl.pallas_call(kernel, out_shape=(pltpu.VMEM(trial.shape, F32), pltpu.VME...]
where the time goes in v2:
time: 38.4 us; the launch traced here: 38.2 us
  Pallas kernels  36.2 us (94%)
  local copies, waits for them, and re-layouts  1.33 us (3%)
  between operations  0.64 us (2%)
    pallas_call x1, Pallas kernels, local(): pl.pallas_call(kernel, out_shape=(pltpu.VMEM(trial.shape, F32), pltpu.VME...  36.2 us
    unnamed x2, local copies, waits for them, and re-layouts  1.33 us

profile of v2, /device:TPU:1, one launch (start us, length us, event | category | flops | bytes accessed | tf_op | source)
XLA Modules:
  0.0 38.2 jit_solution(3447733979221306712)
XLA Ops:
  0.6 36.2 %shard_map.95 = (f32[2,2,4096]{2,1,0:T(2,128)S(1)}, bf16[16,2,4096]{2,1,0:T(2,128)(2,1)S(1)}) custom-call(f32[2,2,4096]{2,1,0:T(2,128)} %trial_in.1, bf16[16,2,4096]{2,1,0:T(2,128)(2,1)} %resident_in.1, f32[4,128,128]{2,1,0:T(8,128)} %potential_in.1, s32[1,128]{1,0:T(1,128)} %bitcast.5, s32[1,4096]{1,0:T(1,128)} %bitcast.3, s32[32]{0:T(128)} %slab_in.1, ...), custom_call_target="tpu_custom_call" | custom-call | flops 4000000000 | bytes 2000000 | tf_op jit(solution)/shard_map/pallas_call | solution.py:395
  36.9 0.6 %copy.12 = f32[2,2,4096]{2,1,0:T(2,128)} copy(f32[2,2,4096]{2,1,0:T(2,128)S(1)} %get-tuple-element.2) | data formatting | bytes 131072
  37.5 0.7 %copy.13 = bf16[16,2,4096]{2,1,0:T(2,128)(2,1)} copy(bf16[16,2,4096]{2,1,0:T(2,128)(2,1)S(1)} %get-tuple-element.3) | data formatting | bytes 524288

commit v3 on v2

--- a/solution.py
+++ b/solution.py
@@ -13,7 +13,10 @@
 CH = 8
 EARLY = 0
 LATE = 2
-PLAN = {"sent": (0,), "start": (1,), "fill1": (2,), "fill3": (3,), "plane0": (4,), "plane1": (5,), "pick5": (6,), "pick10": (7,)}
+RAW = 2
+CUT = CH - RAW
+PLAN = {"sent": (0,), "start": (1,), "fill0": (2,), "fill2": (3,), "fill3": (4,), "plane0": (5,), "end": (6, 7)}
+PASS = {"start": (6,), "fill1": (7,)}
 GR = 4
 MESH = pl.DeviceIdType.MESH
 F32 = jnp.float32
@@ -59,8 +62,8 @@
     applied, rotated,
     trial, resident, potential, columns, cells, slab, owner, rotation, table, loads,
     all_columns, stick_hot, plane_hot, kinetic, sent1, got1, sent2, got2,
-    grid, picked, panels, own_part, part_out, part_in, weight_out, weight_in,
-    col_send, col_recv, s1, r1, s2, r2, xs, xr, zs, zr, ws, wr,
+    grid, picked, panels, others, own_part, part_out, part_in, weight_out, weight_in,
+    col_send, col_recv, s1, r1, s2, r2, xs, xr, zs, zr, ws, wr, fs, fr,
 ):
     col = lax.axis_index("col")
     row = lax.axis_index("row")
@@ -190,6 +193,31 @@
         part_out[c] = r[32:].astype(BF)
         z_copy(c).start()
 
+    def raw_copy(c):
+        return pltpu.make_async_remote_copy(
+            panels.at[c, x], others.at[c - CUT, x], zs.at[c], zr.at[c],
+            device_id=(mate, row), device_id_type=MESH,
+        )
+
+    def pass_copy(c, d, at):
+        return pltpu.make_async_remote_copy(
+            others.at[c - CUT, x], others.at[c - CUT, at], fs.at[c - CUT, d - 1], fr.at[c - CUT, d - 1],
+            device_id=(x_peer(d), row), device_id_type=MESH,
+        )
+
+    def pass_on(c):
+        raw_copy(c).wait_recv()
+        for d in (2, 1, 3):
+            pass_copy(c, d, x).start()
+
+    def rotate_raw(c):
+        for d in range(1, XS):
+            x_arrival(c, d).wait_recv()
+            pass_copy(c, d, lax.rem(x + XS - d, XS)).wait_recv()
+        r = dot(weight_own, panels[c].reshape(4 * 32, width))
+        r = r + dot(weight_out[...], others[c - CUT].reshape(4 * 32, width))
+        rotated[:, :, c * width:(c + 1) * width] = r.astype(BF).reshape(16, 2, width)
+
     def z_copy(c):
         return pltpu.make_async_remote_copy(
             part_out.at[c], part_in.at[c], zs.at[c], zr.at[c],
@@ -197,8 +225,10 @@
         )
 
     def rotations(place):
+        for c in PASS.get(place, ()):
+            pass_on(c)
         for c in PLAN.get(place, ()):
-            rotate(c)
+            (rotate if c < CUT else rotate_raw)(c)
 
     def send_column(q, i, to):
         pltpu.make_async_remote_copy(
@@ -206,6 +236,8 @@
             device_id=(col, to), device_id_type=MESH,
         ).start()
 
+    for c in range(CUT, CH):
+        raw_copy(c).start()
     for d in (2, 1, 3):
         x_copy(0, d).start()
     send_column(0, 0, sibling)
@@ -371,8 +403,9 @@
                 [jnp.sum(jnp.where(hit, u[(2 * s + p) * 64:(2 * s + p + 1) * 64], 0.0),
                          axis=0, keepdims=True) for p in range(2)], axis=0)
             applied[s, :, at] = v + kin * trial[s, :, at]
-
-    for c in range(CH):
+    rotations("last")
+
+    for c in range(CUT):
         z_copy(c).wait_recv()
         total = own_part[c] + part_in[c].astype(F32)
         rotated[:, :, c * width:(c + 1) * width] = total.astype(BF).reshape(16, 2, width)
@@ -383,7 +416,9 @@
     for c in range(CH):
         for d in range(1, XS):
             x_copy(c, d).wait_send()
-        z_copy(c).wait_send()
+            if c >= CUT:
+                pass_copy(c, d, x).wait_send()
+        (z_copy if c < CUT else raw_copy)(c).wait_send()
 
 
 def local(trial, resident, potential, columns, cells, slab, owner, rotation):
@@ -422,6 +457,7 @@
             pltpu.VMEM((1024, 256), F32),
             pltpu.VMEM((1024, 256), BF),
             pltpu.VMEM((CH, XS, 32, width), BF),
+            pltpu.VMEM((RAW, XS, 32, width), BF),
             pltpu.VMEM((CH, 32, width), F32),
             pltpu.VMEM((CH, 32, width), BF),
             pltpu.VMEM((CH, 32, width), BF),
@@ -429,6 +465,7 @@
             pltpu.VMEM((32, NG), BF),
             dma, dma, dma, dma((GR,)), dma, dma,
             dma((CH, XS - 1)), dma((CH, XS - 1)), dma((CH,)), dma((CH,)), dma, dma,
+            dma((RAW, XS - 1)), dma((RAW, XS - 1)),
         ],
         compiler_params=pltpu.CompilerParams(
             collective_id=0, has_side_effects=True, vmem_limit_bytes=48 * 2**20

time: 38.4 us -> 36.1 us (0.940)
  Pallas kernels: 36.2 us -> 34 us
    pallas_call x1, Pallas kernels: 36.2 us -> 34 us  [local(): pl.pallas_call(kernel, out_shape=(pltpu.VMEM(trial.shape, F32), pltpu.VME...]
where the time goes in v3:
time: 36.1 us; the launch traced here: 36 us
  Pallas kernels  34 us (94%)
  local copies, waits for them, and re-layouts  1.33 us (4%)
  between operations  0.64 us (2%)
    pallas_call x1, Pallas kernels, local(): pl.pallas_call(kernel, out_shape=(pltpu.VMEM(trial.shape, F32), pltpu.VME...  34 us
    unnamed x2, local copies, waits for them, and re-layouts  1.33 us

profile of v3, /device:TPU:1, one launch (start us, length us, event | category | flops | bytes accessed | tf_op | source)
XLA Modules:
  0.0 36.0 jit_solution(8402830689572050773)
XLA Ops:
  0.6 34.0 %shard_map.95 = (f32[2,2,4096]{2,1,0:T(2,128)S(1)}, bf16[16,2,4096]{2,1,0:T(2,128)(2,1)S(1)}) custom-call(f32[2,2,4096]{2,1,0:T(2,128)} %trial_in.1, bf16[16,2,4096]{2,1,0:T(2,128)(2,1)} %resident_in.1, f32[4,128,128]{2,1,0:T(8,128)} %potential_in.1, s32[1,128]{1,0:T(1,128)} %bitcast.5, s32[1,4096]{1,0:T(1,128)} %bitcast.3, s32[32]{0:T(128)} %slab_in.1, ...), custom_call_target="tpu_custom_call" | custom-call | flops 4000000000 | bytes 2000000 | tf_op jit(solution)/shard_map/pallas_call | solution.py:430
  34.6 0.6 %copy.12 = f32[2,2,4096]{2,1,0:T(2,128)} copy(f32[2,2,4096]{2,1,0:T(2,128)S(1)} %get-tuple-element.2) | data formatting | bytes 131072
  35.3 0.7 %copy.13 = bf16[16,2,4096]{2,1,0:T(2,128)(2,1)} copy(bf16[16,2,4096]{2,1,0:T(2,128)(2,1)S(1)} %get-tuple-element.3) | data formatting | bytes 524288

commit v4 on v3

--- a/solution.py
+++ b/solution.py
@@ -15,8 +15,8 @@
 LATE = 2
 RAW = 2
 CUT = CH - RAW
-PLAN = {"sent": (0,), "start": (1,), "fill0": (2,), "fill2": (3,), "fill3": (4,), "plane0": (5,), "end": (6, 7)}
-PASS = {"start": (6,), "fill1": (7,)}
+PLAN = {"start": (0, 1), "fill0": (2,), "fill1": (3,), "fill2": (4,), "fill3": (5,), "end": (6, 7)}
+PASS = {"fill1": (6,), "fill3": (7,)}
 GR = 4
 MESH = pl.DeviceIdType.MESH
 F32 = jnp.float32

time: 36.1 us -> 35.7 us (0.989)
  Pallas kernels: 34 us -> 33.6 us
    pallas_call x1, Pallas kernels: 34 us -> 33.6 us  [local(): pl.pallas_call(kernel, out_shape=(pltpu.VMEM(trial.shape, F32), pltpu.VME...]
where the time goes in v4:
time: 35.7 us; the launch traced here: 35.6 us
  Pallas kernels  33.6 us (94%)
  local copies, waits for them, and re-layouts  1.33 us (4%)
  between operations  0.64 us (2%)
    pallas_call x1, Pallas kernels, local(): pl.pallas_call(kernel, out_shape=(pltpu.VMEM(trial.shape, F32), pltpu.VME...  33.6 us
    unnamed x2, local copies, waits for them, and re-layouts  1.33 us

profile of v4, /device:TPU:1, one launch (start us, length us, event | category | flops | bytes accessed | tf_op | source)
XLA Modules:
  0.0 35.6 jit_solution(16817715590322518777)
XLA Ops:
  0.6 33.6 %shard_map.95 = (f32[2,2,4096]{2,1,0:T(2,128)S(1)}, bf16[16,2,4096]{2,1,0:T(2,128)(2,1)S(1)}) custom-call(f32[2,2,4096]{2,1,0:T(2,128)} %trial_in.1, bf16[16,2,4096]{2,1,0:T(2,128)(2,1)} %resident_in.1, f32[4,128,128]{2,1,0:T(8,128)} %potential_in.1, s32[1,128]{1,0:T(1,128)} %bitcast.5, s32[1,4096]{1,0:T(1,128)} %bitcast.3, s32[32]{0:T(128)} %slab_in.1, ...), custom_call_target="tpu_custom_call" | custom-call | flops 4000000000 | bytes 2000000 | tf_op jit(solution)/shard_map/pallas_call | solution.py:430
  34.3 0.6 %copy.12 = f32[2,2,4096]{2,1,0:T(2,128)} copy(f32[2,2,4096]{2,1,0:T(2,128)S(1)} %get-tuple-element.2) | data formatting | bytes 131072
  34.9 0.7 %copy.13 = bf16[16,2,4096]{2,1,0:T(2,128)(2,1)} copy(bf16[16,2,4096]{2,1,0:T(2,128)(2,1)S(1)} %get-tuple-element.3) | data formatting | bytes 524288

commit v5 on v4

--- a/solution.py
+++ b/solution.py
@@ -120,11 +120,10 @@
         z = cell // NG
         hot = onehot((z // 64) * NG + cell % NG, 256)
         stick_hot[:, at] = hot
-        hit = lax.broadcasted_iota(jnp.int32, (64, 512), 0) == z % 64
+        deep = onehot(z % 64, 64)
         left = jnp.concatenate(
-            [jnp.where(hit, trial[s, p:p + 1, at], 0.0) for s in range(2) for p in range(2)],
-            axis=0,
-        ).astype(BF)
+            [deep * trial[s, p:p + 1, at].astype(BF) for s in range(2) for p in range(2)], axis=0
+        )
         return dot_nt(left, hot)
 
     def sticks(first, last, acc=None):
@@ -308,13 +307,13 @@
     for g in range(GR):
         pltpu.make_async_copy(got1.at[pl.ds(g * per, per)], got1.at[pl.ds(g * per, per)], r1.at[g]).wait()
         key = jnp.concatenate([all_columns[per * g + i] for i in range(per)], axis=1)
-        hit = lax.broadcasted_iota(jnp.int32, (64, per * NG), 0) == key // NG % 64
-        values = jnp.concatenate([got1[per * g + i] for i in range(per)], axis=1).astype(F32)
+        across = onehot(key // NG % 64, 64)
+        values = jnp.concatenate([got1[per * g + i] for i in range(per)], axis=1)
         right = plane_hot[:, g * per * NG:(g + 1) * per * NG]
         for m in range(4):
             left = jnp.concatenate(
-                [jnp.where(hit, values[4 * m + i:4 * m + i + 1], 0.0) for i in range(4)], axis=0
-            ).astype(BF)
+                [across * values[4 * m + i:4 * m + i + 1] for i in range(4)], axis=0
+            )
             part = dot_nt(left, right)
             if g == 0:
                 grid[256 * m:256 * m + 256] = part

time: 35.7 us -> 35.7 us (level)
  no operation moved by 1% of the time
where the time goes in v5:
time: 35.7 us; the launch traced here: 35.6 us
  Pallas kernels  33.6 us (94%)
  local copies, waits for them, and re-layouts  1.33 us (4%)
  between operations  0.64 us (2%)
    pallas_call x1, Pallas kernels, local(): pl.pallas_call(kernel, out_shape=(pltpu.VMEM(trial.shape, F32), pltpu.VME...  33.6 us
    unnamed x2, local copies, waits for them, and re-layouts  1.33 us

profile of v5, /device:TPU:1, one launch (start us, length us, event | category | flops | bytes accessed | tf_op | source)
XLA Modules:
  0.0 35.6 jit_solution(749813123508984000)
XLA Ops:
  0.6 33.6 %shard_map.95 = (f32[2,2,4096]{2,1,0:T(2,128)S(1)}, bf16[16,2,4096]{2,1,0:T(2,128)(2,1)S(1)}) custom-call(f32[2,2,4096]{2,1,0:T(2,128)} %trial_in.1, bf16[16,2,4096]{2,1,0:T(2,128)(2,1)} %resident_in.1, f32[4,128,128]{2,1,0:T(8,128)} %potential_in.1, s32[1,128]{1,0:T(1,128)} %bitcast.5, s32[1,4096]{1,0:T(1,128)} %bitcast.3, s32[32]{0:T(128)} %slab_in.1, ...), custom_call_target="tpu_custom_call" | custom-call | flops 4000000000 | bytes 2000000 | tf_op jit(solution)/shard_map/pallas_call | solution.py:429
  34.2 0.6 %copy.12 = f32[2,2,4096]{2,1,0:T(2,128)} copy(f32[2,2,4096]{2,1,0:T(2,128)S(1)} %get-tuple-element.2) | data formatting | bytes 131072
  34.9 0.7 %copy.13 = bf16[16,2,4096]{2,1,0:T(2,128)(2,1)} copy(bf16[16,2,4096]{2,1,0:T(2,128)(2,1)S(1)} %get-tuple-element.3) | data formatting | bytes 524288
